TPU v7x, 32 devices: a whole 2x2x4 slice. The times are simulated.
32 devices in a mesh: groups: 2 (over y), hidden: 8 (over z, core), mp: 2 (over x).
Axes of the slice: x: 2, y: 2, z: 4, core: 2. Of those that a mesh axis runs over, the one named last changes fastest.
Arguments:
- stream_rows: bfloat16 [64, 2, 16384], P(('groups', 'hidden'), None, 'mp'), parts along dimension 0, may hold values from -6 to 6
- norm_gain: bfloat16 [16384], P('mp'), may hold values from 0.5 to 1.5
- query_weight: bfloat16 [16384, 8, 1024], P('hidden', 'mp'), may hold values from -0.046875 to 0.046875
- keyval_weight: bfloat16 [16384, 8, 256], P('hidden', 'mp'), may hold values from -0.046875 to 0.046875
- output_weight: bfloat16 [8, 1024, 16384], P('mp', None, 'hidden'), may hold values from -0.25 to 0.25
- key_cache: bfloat16 [64, 8, 1024, 128], P(('groups', 'hidden'), 'mp'), parts along dimension 0, may hold values from -400 to 400
- value_cache: bfloat16 [64, 8, 1024, 128], P(('groups', 'hidden'), 'mp'), parts along dimension 0, may hold values from -6 to 6
- lengths: int32 [64], P(('groups', 'hidden')), parts along dimension 0, may hold values from 128 to 1024, as said below
Outputs:
- branch: bfloat16 [64, 2, 16384], P(('groups', 'mp'), None, 'hidden'), parts along dimension 0
There are 2 independent parts, one for each index of `groups`. A program takes and returns all parts, laid end to end along the dimension named above; an argument that names none is the same for every part. Nothing has to cross between parts.
Inputs may be any that keep to these rules, and one draw needn't show every extreme that they name: `lengths`: in each group, one sequence has exactly 1024 filled slots and one exactly 128.
All inputs are finite; a program needn't handle non-finite values.
Results may differ from a plain program's by a relative error of at most 0.0055.
The roundings to bfloat16 on the way count: a program that leaves them out, or rounds other values in their place, can miss the bound.
Values may be sent and summed in bfloat16 or wider, within the bound.
A program may use at most 192 MiB of HBM per device.

v0:
```python
import math

import jax
import jax.numpy as jnp
from jax import lax
from jax.sharding import PartitionSpec as P

rope_base = 500000.0


def norm_blocks(pieces, gains, blocks):
    values = pieces.astype(jnp.float32)
    scale = lax.rsqrt(jnp.mean(values * values, axis=(0, 3), keepdims=True) + 1e-05)
    scaled = values * scale * gains.astype(jnp.float32)[:, None, None, :]
    width_parts, seqs, steps_all, narrow = scaled.shape
    whole = jnp.transpose(scaled, (1, 2, 0, 3)).reshape(
        seqs, steps_all, blocks, width_parts * narrow // blocks
    )
    return jnp.transpose(whole, (2, 0, 1, 3)).astype(jnp.bfloat16)


def rotate(values, pos):
    half = values.shape[-1] // 2
    freq = jnp.exp(
        jnp.arange(half, dtype=jnp.float32) * (-2.0 * math.log(rope_base) / values.shape[-1])
    )
    angle = pos[..., None] * freq
    cosine = jnp.cos(angle)
    sine = jnp.sin(angle)
    first = values[..., :half]
    second = values[..., half:]
    return jnp.concatenate(
        [first * cosine - second * sine, second * cosine + first * sine], axis=-1
    )


def attend(query, new_keys, new_vals, key_cache, value_cache, lengths, step, width, count):
    scale = query.shape[-1] ** (-0.5)
    fresh = (
        jnp.einsum("sgqd,stgd->sgqt", query, new_keys, preferred_element_type=jnp.float32) * scale
    )
    keep = jnp.arange(new_keys.shape[1]) <= step
    fresh = jnp.where(keep, fresh, -jnp.inf)

    def block_scores(index):
        scores = (
            jnp.einsum("sgqd,sgkd->sgqk", query, key_cache, preferred_element_type=jnp.float32)
            * scale
        )
        slots = (index * width + jnp.arange(width))[None, :] < lengths[:, None]
        return (scores, slots[:, None, None, :])

    def widen(index, top):
        scores, slots = block_scores(index)
        return jnp.maximum(top, jnp.max(jnp.where(slots, scores, -jnp.inf), axis=-1))

    top = lax.fori_loop(0, count, widen, jnp.max(fresh, axis=-1))
    p_fresh = jnp.where(keep, jnp.exp(fresh - top[..., None]), 0.0)
    total = jnp.sum(p_fresh, axis=-1)
    acc = jnp.einsum(
        "sgqt,stgd->sgqd",
        p_fresh.astype(jnp.bfloat16),
        new_vals,
        preferred_element_type=jnp.float32,
    )

    def accumulate(index, carry):
        acc_now, total_now = carry
        scores, slots = block_scores(index)
        weights = jnp.where(slots, jnp.exp(scores - top[..., None]), 0.0)
        acc_now = acc_now + jnp.einsum(
            "sgqk,sgkd->sgqd",
            weights.astype(jnp.bfloat16),
            value_cache,
            preferred_element_type=jnp.float32,
        )
        return (acc_now, total_now + jnp.sum(weights, axis=-1))

    acc, total = lax.fori_loop(0, count, accumulate, (acc, total))
    return (acc / total[..., None]).astype(jnp.bfloat16)


def local(
    stream_rows,
    norm_gain,
    query_weight,
    keyval_weight,
    output_weight,
    key_cache,
    value_cache,
    lengths,
):
    seqs = stream_rows.shape[0]
    steps_all = stream_rows.shape[1]
    narrow = stream_rows.shape[2]
    pieces, gains = (
        lax.all_gather(stream_rows.reshape(1, seqs, steps_all, narrow), "mp", axis=0, tiled=True),
        lax.all_gather(norm_gain.reshape(1, narrow), "mp", axis=0, tiled=True),
    )
    blocks = lax.axis_size("hidden")
    normed = norm_blocks(pieces, gains, blocks)
    block = query_weight.shape[0]
    groups_here = query_weight.shape[1]
    head = keyval_weight.shape[2] // 2
    per_group = query_weight.shape[2] // head
    q_cols = groups_here * per_group * head
    wq_flat = query_weight.reshape(block, q_cols)
    wkv_flat = keyval_weight.reshape(block, groups_here * 2 * head)
    wo_flat = output_weight.reshape(q_cols, output_weight.shape[2])
    spread = lax.all_to_all(normed, "hidden", split_axis=0, concat_axis=0, tiled=True)
    spread = spread.reshape(blocks * seqs, steps_all, block)
    piece = spread
    flat = piece.reshape(-1, block)
    q_part = jnp.dot(flat, wq_flat, preferred_element_type=jnp.float32)
    kv_part = jnp.dot(flat, wkv_flat, preferred_element_type=jnp.float32)
    joined = jnp.concatenate([q_part, kv_part], axis=1)
    sums = lax.psum_scatter(
        joined.reshape(piece.shape[:-1] + (joined.shape[-1],)),
        "hidden",
        scatter_dimension=0,
        tiled=True,
    )
    qraw = sums[..., :q_cols].reshape(seqs, steps_all, groups_here, per_group, head)
    kvraw = sums[..., q_cols:].reshape(seqs, steps_all, groups_here, 2, head)
    pos = (lengths[:, None] + jnp.arange(steps_all, dtype=jnp.int32)[None, :]).astype(jnp.float32)
    query = rotate(qraw, pos[:, :, None, None]).astype(jnp.bfloat16)
    new_keys = rotate(kvraw[:, :, :, 0, :], pos[:, :, None]).astype(jnp.bfloat16)
    new_vals = kvraw[:, :, :, 1, :].astype(jnp.bfloat16)
    slots_all = key_cache.shape[2]
    count = 1
    results = []
    for step in range(steps_all):
        heads = attend(
            query[:, step],
            new_keys,
            new_vals,
            key_cache,
            value_cache,
            lengths,
            step,
            slots_all,
            count,
        )
        results.append(heads.reshape(seqs, q_cols))
    heads_all = jnp.stack(results, axis=1)
    piece = lax.all_gather(heads_all, "hidden", axis=0, tiled=True)
    flat = piece.reshape(-1, q_cols)
    product = jnp.dot(flat, wo_flat, preferred_element_type=jnp.float32)
    partial_value = product.reshape(piece.shape[:-1] + (wo_flat.shape[1],))
    return lax.psum_scatter(partial_value, "mp", scatter_dimension=0, tiled=True).astype(
        jnp.bfloat16
    )


def solution(mesh):
    in_specs = (
        P(("groups", "hidden"), None, "mp"),
        P("mp"),
        P("hidden", "mp", None),
        P("hidden", "mp", None),
        P("mp", None, "hidden"),
        P(("groups", "hidden"), "mp", None, None),
        P(("groups", "hidden"), "mp", None, None),
        P(("groups", "hidden")),
    )
    out_specs = P(("groups", "mp"), None, "hidden")
    return jax.shard_map(local, mesh=mesh, in_specs=in_specs, out_specs=out_specs, check_vma=False)
```

profile of v0, /device:TPU:0, one launch (start us, length us, event | category | flops | bytes accessed | tf_op | source)
XLA Modules:
  0.0 177.1 jit_solution(13549066770180057497)
XLA Ops:
  6.5 7.4 %all-gather = bf16[8,2,8192]{2,1,0:T(2,128)(2,1)S(1)} all-gather(bf16[4,2,8192]{2,1,0:T(2,128)(2,1)} %param.8), channel_id=2, replica_groups=mesh['groups'=2,'hidden'=8,'mp'=2] {'mp'}, dimensions={0}, use_global_device_ids=true | all-gather | bytes 393216 | tf_op jit(solution)/shard_map/all_gather | solution.py:97
  14.1 0.4 multiply_reduce_fusion
  14.5 4.6 %all-gather.1 = bf16[16384]{0:T(1024)(128)(2,1)S(1)} all-gather(bf16[8192]{0:T(1024)(128)(2,1)} %param.9), channel_id=3, replica_groups=mesh['groups'=2,'hidden'=8,'mp'=2] {'mp'}, dimensions={0}, use_global_device_ids=true | all-gather | bytes 49152 | tf_op jit(solution)/shard_map/all_gather | solution.py:98
  19.2 0.5 fusion.22
  19.7 1.0 copy.22
  20.7 5.1 %all-to-all-start = ((bf16[8,4,2,2048]{3,2,1,0:T(2,128)(2,1)}), bf16[8,4,2,2048]{3,2,1,0:T(2,128)(2,1)S(1)}, u32[]{:S(2)}, u32[]{:S(2)}) async-start(bf16[8,4,2,2048]{3,2,1,0:T(2,128)(2,1)} %copy.22), calls=%async_computation | async-start | bytes 524288 | tf_op jit(solution)/shard_map/all_to_all | solution.py:110
  25.8 17.2 %copy.37 = bf16[256,8,4,1024]{3,1,2,0:T(8,128)(2,1)} copy(bf16[256,8,4,1024]{3,2,1,0:T(4,128)(2,1)} %bitcast.48) | data formatting | bytes 33554432
  43.0 3.0 %copy.38 = bf16[256,8,4,256]{3,1,2,0:T(8,128)(2,1)} copy(bf16[256,8,4,256]{3,2,1,0:T(4,128)(2,1)S(1)} %bitcast.50) | data formatting | bytes 8388608
  46.2 8.9 %fusion.42 = f32[64,4096]{1,0:T(8,128)S(1)} fusion(bf16[64,2048]{1,0:T(8,128)(2,1)S(1)} %reshape_reshape.3, bf16[2048,4096]{1,0:T(8,128)(2,1)} %bitcast.46), kind=kOutput, calls=%fused_computation.73 | convolution fusion | flops 1073741824 | bytes 18087936 | tf_op jit(solution)/shard_map/dot_general | solution.py:114
  55.1 0.8 fusion.43
  56.1 1.9 %reshape.151 = f32[32,2,5120]{2,1,0:T(2,128)} reshape(f32[64,5120]{1,0:T(8,128)S(1)} %pad_maximum_fusion) | data formatting | bytes 2621440 | tf_op jit(solution)/shard_map/reshape | solution.py:118
  58.4 0.6 dynamic-slice
  59.7 59.9 %all-reduce.3.cloned.1.call-done = f32[32,2,5120]{2,1,0:T(2,128)} async-done(((f32[32,2,5120]{2,1,0:T(2,128)}), f32[32,2,5120]{2,1,0:T(2,128)}) %all-reduce.3.cloned.1.call-update) | async-done | bytes 1310736
  119.7 0.8 constant_dynamic-slice_fusion.1
  120.6 0.9 constant_dynamic-slice_fusion
  122.0 3.7 %select_reduce_fusion.1 = (f32[4,4,8]{2,1,0:T(4,128)S(1)}, f32[4,4,8,1024]{3,2,1,0:T(8,128)S(1)}) fusion(pred[4,1024]{1,0:T(4,128)(4,1)S(1)} %iota_compare_fusion, bf16[4,4,1024,128]{3,2,1,0:T(8,128)(2,1)} %param.13, bf16[4,2,4,8,64]{4,3,2,0,1:T(8,128)(2,1)S(1)} %get-tuple-element.65, bf16[4,2,4,8,64]{4,3,2,0,1:T(8,128)(2,1)S(1)} %get-tuple-element.72), kind=kOutput, calls=%fused_computation.21 | convolution fusion | flops 34013056 | bytes 4788736 | tf_op jit(solution)/shard_map/while/body/eval_jaxpr/sgqd,sgkd->sgqk/dot_general | solution.py:47
  126.2 1.3 fusion.10
  127.5 0.7 fusion.16
  128.5 0.7 fusion.14
  130.2 14.8 %all_gather.11 = bf16[32,2,4096]{2,1,0:T(2,128)(2,1)S(1)} all-gather(bf16[4,2,4096]{2,1,0:T(2,128)(2,1)S(1)} %pad_maximum_fusion.1), channel_id=1, replica_groups=mesh['groups'=2,'hidden'=8,'mp'=2] {'hidden'}, dimensions={0}, use_global_device_ids=true | all-gather | bytes 589824 | tf_op jit(solution)/shard_map/all_gather | solution.py:146
  145.0 9.7 %fusion.6 = f32[32,2,2048]{2,0,1:T(8,128)} fusion(bf16[4096,2048,1]{1,0,2:T(8,128)(2,1)} %bitcast.47, bf16[32,2,4096]{2,1,0:T(2,128)(2,1)S(1)} %all_gather.11), kind=kOutput, calls=%fused_computation.13 | convolution fusion | flops 1073741824 | bytes 17825792 | tf_op jit(solution)/shard_map/dot_general | solution.py:148
  154.8 13.7 %reduce-scatter.2.cloned.1.call-done = f32[16,2,2048]{2,0,1:T(8,128)} async-done(((f32[32,2,2048]{2,0,1:T(8,128)}), f32[16,2,2048]{2,0,1:T(8,128)}) %reduce-scatter.2.cloned.1.call-update) | async-done | bytes 262160 | tf_op jit(solution)/shard_map/reduce_scatter | solution.py:150
  168.5 1.0 convert_element_type.72
  169.4 0.8 copy.31
  (53 shorter events, 3.3 us)
Async XLA Ops:
  20.7 25.4 %all-to-all-start = ((bf16[8,4,2,2048]{3,2,1,0:T(2,128)(2,1)}), bf16[8,4,2,2048]{3,2,1,0:T(2,128)(2,1)S(1)}, u32[]{:S(2)}, u32[]{:S(2)}) async-start(bf16[8,4,2,2048]{3,2,1,0:T(2,128)(2,1)} %copy.22), calls=%async_computation | async-start | bytes 524288 | tf_op jit(solution)/shard_map/all_to_all | solution.py:110
  25.8 93.9 %all-reduce.3.cloned.1.call-start = ((), (), s32[]{:S(2)}) async-start(), calls=%async_computation.3 | async-start | bytes 2621440
  25.8 17.2 %copy-start.3 = (bf16[2048,4,256]{2,1,0:T(4,128)(2,1)S(1)}, bf16[2048,4,256]{2,1,0:T(4,128)(2,1)}, u32[]{:S(2)}) copy-start(bf16[2048,4,256]{2,1,0:T(4,128)(2,1)} %param.11) | copy-start | bytes 12582916
  43.0 3.0 %copy-start.4 = (s32[4]{0:T(128)S(1)}, s32[4]{0:T(128)}, u32[]{:S(2)}) copy-start(s32[4]{0:T(128)} %param.15) | copy-start | bytes 52
  46.2 9.0 %copy-start.2 = (bf16[256,8,4,256]{3,1,2,0:T(8,128)(2,1)S(1)}, bf16[256,8,4,256]{3,1,2,0:T(8,128)(2,1)}, u32[]{:S(2)}) copy-start(bf16[256,8,4,256]{3,1,2,0:T(8,128)(2,1)} %copy.38) | copy-start | bytes 12582916
  56.0 2.4 %copy-start.5 = (u32[32]{0:T(128)S(1)}, u32[32]{0:T(128)}, u32[]{:S(2)}) copy-start(u32[32]{0:T(128)} %constant.60) | copy-start | bytes 388
  58.0 110.5 %reduce-scatter.2.cloned.1.call-start = ((), (), s32[]{:S(2)}) async-start(), calls=%async_computation.2 | async-start | bytes 786432 | tf_op jit(solution)/shard_map/reduce_scatter | solution.py:150
  121.7 4.6 %copy-start.1 = (bf16[4,4,1024,128]{3,2,1,0:T(8,128)(2,1)S(1)}, bf16[4,4,1024,128]{3,2,1,0:T(8,128)(2,1)}, u32[]{:S(2)}) copy-start(bf16[4,4,1024,128]{3,2,1,0:T(8,128)(2,1)} %param.13) | copy-start | bytes 12582916
  122.0 5.5 %copy-start = (bf16[4,4,1024,128]{3,2,1,0:T(8,128)(2,1)S(1)}, bf16[4,4,1024,128]{3,2,1,0:T(8,128)(2,1)}, u32[]{:S(2)}) copy-start(bf16[4,4,1024,128]{3,2,1,0:T(8,128)(2,1)} %param.14) | copy-start | bytes 12582916
Sparse Core Ops, SparseCore 0:
  58.1 61.5 all-reduce.2
  154.9 13.5 reduce-scatter.1
where the time goes:
time: 178 us; the launch traced here: 177 us
  waiting for transfers between devices  73.7 us (41%)
  matrix products  27 us (15%)
  blocking collectives  26.8 us (15%)
  local copies, waits for them, and re-layouts  26.7 us (15%)
  between operations  14.4 us (8%)
  starting transfers between devices  5.35 us (3%)
  other arithmetic  3.24 us (2%)
    unnamed x3, waiting for transfers between devices  60 us
    unnamed x16, local copies, waits for them, and re-layouts  20.8 us
    all_gather x1, blocking collectives, local(): piece = lax.all_gather(heads_all, 'hidden', axis=0, tiled=True)  14.8 us
    reduce_scatter x1, waiting for transfers between devices, local(): lax.psum_scatter(partial_value, 'mp', scatter_dimension=0, tiled=True)  13.7 us
    dot_general x1, matrix products, local(): product = jnp.dot(flat, wo_flat, preferred_element_type=jnp.float32)  9.73 us
    dot_general x1, matrix products, local(): q_part = jnp.dot(flat, wq_flat, preferred_element_type=jnp.float32)  8.93 us
    all_gather x1, blocking collectives, local(): lax.all_gather(stream_rows.reshape(1, seqs, steps_all, narrow), 'mp', axi...  7.35 us
    all_to_all x1, starting transfers between devices, local(): lax.all_to_all(normed, 'hidden', split_axis=0, concat_axis=0, tiled=True)  5.09 us
  transfers between devices with their start and end apart: 3, of which 2 were waited for; matrix products, arithmetic and copies ran while one was open for 12% of the time, Pallas kernels for 0%

commit v1 on v0

--- a/solution.py
+++ b/solution.py
@@ -1,8 +1,11 @@
+import functools
 import math
 
 import jax
 import jax.numpy as jnp
 from jax import lax
+from jax.experimental import pallas as pl
+from jax.experimental.pallas import tpu as pltpu
 from jax.sharding import PartitionSpec as P
 
 rope_base = 500000.0
@@ -152,6 +155,438 @@
     )
 
 
+def fused_kernel(
+    xb, gain, trig, lens, wq, wkv, wo, kcache, vcache, out,
+    xr, ssl, ssr, gbuf, xexp, wbuf, kbuf, vbuf, obuf_w, part, recv1, recv2, hbuf, acc, osend, orecv,
+    xsend_sem, xsem, ss_send, ss_sem, gsem, wsem, csem, wosem,
+    s1_send, s1_sem, s2_send, s2_sem, h_send, h_sem, f_send, f_sem, o_send, o_sem,
+    *, hidden, mp, width,
+):
+    gy = lax.axis_index("groups")
+    h = lax.axis_index("hidden")
+    m = lax.axis_index("mp")
+    z = h // 2
+    c = h % 2
+    zs = hidden // 2
+    nb, rows, block = xb.shape
+    heads_here = wq.shape[1]
+    head = kcache.shape[3]
+    qper = wq.shape[2] // head
+    slots = kcache.shape[2]
+    chunks = (qper + 2) // 2
+    all_rows = hidden * rows
+    depth = block * heads_here
+
+    def at(hh, mm):
+        return (gy, hh, mm)
+
+    def remote(src, dst, send, recv, hh, mm):
+        return pltpu.make_async_remote_copy(
+            src_ref=src, dst_ref=dst, send_sem=send, recv_sem=recv,
+            device_id=at(hh, mm), device_id_type=pl.DeviceIdType.MESH,
+        )
+
+    def arrived(ref, sem):
+        pltpu.make_async_copy(ref, ref, sem).wait()
+
+    weight_copies = []
+    for j in range(qper + 2):
+        if j < 2:
+            src = wkv.at[:, :, pl.ds(j * head, head)]
+        else:
+            src = wq.at[:, :, pl.ds((j - 2) * head, head)]
+        copy = pltpu.make_async_copy(src, wbuf.at[j], wsem.at[j])
+        copy.start()
+        weight_copies.append(copy)
+
+    barrier = pltpu.get_barrier_semaphore()
+    for dh in range(hidden):
+        for dm in range(mp):
+            if dh or dm:
+                pl.semaphore_signal(
+                    barrier, inc=1, device_id=at((h + dh) % hidden, (m + dm) % mp),
+                    device_id_type=pl.DeviceIdType.MESH,
+                )
+    pl.semaphore_wait(barrier, hidden * mp - 1)
+
+    row_sends = []
+    for b in range(nb):
+        for dm in range(mp):
+            hh = m * nb + b
+            mm = (m + dm) % mp
+            copy = remote(
+                xb.at[b], xr.at[h], xsend_sem.at[b * mp + dm], xsem.at[h], hh, mm
+            )
+            if dm == 0:
+                mine = hh == h
+                local_copy = pltpu.make_async_copy(xb.at[b], xr.at[h], xsem.at[h])
+
+                @pl.when(mine)
+                def _(local_copy=local_copy):
+                    local_copy.start()
+
+                @pl.when(jnp.logical_not(mine))
+                def _(copy=copy):
+                    copy.start()
+
+                row_sends.append((copy, mine))
+            else:
+                copy.start()
+                row_sends.append((copy, None))
+
+    holder = h // nb == m
+    gain_copy = remote(gain.at[h % nb], gbuf, gsem.at[0], gsem.at[1], h, (m + 1) % mp)
+    gain_local = pltpu.make_async_copy(gain.at[h % nb], gbuf, gsem.at[2])
+
+    @pl.when(holder)
+    def _():
+        gain_copy.start()
+        gain_local.start()
+
+    values = xb[...].astype(jnp.float32)
+    squares = jnp.sum(jnp.sum(values * values, axis=0), axis=-1, keepdims=True)
+    ssl[...] = jnp.broadcast_to(squares, ssl.shape)
+    ssr[m, h] = ssl[...]
+    ss_sends = []
+    for dh in range(hidden):
+        for dm in range(mp):
+            if dh or dm:
+                copy = remote(
+                    ssl, ssr.at[m, h], ss_send.at[dh * mp + dm], ss_sem.at[m, h],
+                    (h + dh) % hidden, (m + dm) % mp,
+                )
+                copy.start()
+                ss_sends.append(copy)
+
+    cache_copies = []
+    for g in range(heads_here):
+        pair = (
+            pltpu.make_async_copy(kcache.at[:, g], kbuf.at[:, g], csem.at[0, g]),
+            pltpu.make_async_copy(vcache.at[:, g], vbuf.at[:, g], csem.at[1, g]),
+        )
+        for copy in pair:
+            copy.start()
+        cache_copies.append(pair)
+    out_copies = []
+    for g in range(heads_here):
+        copy = pltpu.make_async_copy(wo.at[g], obuf_w.at[g], wosem.at[g])
+        copy.start()
+        out_copies.append(copy)
+
+    for dh in range(hidden):
+        for dm in range(mp):
+            if dh or dm:
+                hh = (h + dh) % hidden
+                mm = (m + dm) % mp
+                arrived(ssr.at[mm, hh], ss_sem.at[mm, hh])
+
+    @pl.when(holder)
+    def _():
+        gain_local.wait()
+        gain_copy.wait_send()
+
+    @pl.when(jnp.logical_not(holder))
+    def _():
+        gain_copy.wait_recv()
+
+    for src in range(hidden):
+        arrived(xr.at[src], xsem.at[src])
+    total_sq = jnp.sum(ssr[...], axis=0).reshape(all_rows, ssl.shape[1])
+    scale = lax.rsqrt(total_sq / (nb * mp * block) + 1e-05)[:, :1]
+    rows_f = xr[...].astype(jnp.float32).reshape(all_rows, block)
+    normed = (rows_f * scale * gbuf[...]).astype(jnp.bfloat16)
+
+    lane = 128
+    wide = lane * heads_here
+    row_of = lax.broadcasted_iota(jnp.int32, (lane, wide), 0)
+    col_of = lax.broadcasted_iota(jnp.int32, (lane, wide), 1)
+    spread = jnp.where(col_of // heads_here == row_of, 1.0, 0.0).astype(jnp.bfloat16)
+    which = lax.broadcasted_iota(jnp.int32, (all_rows, wide), 1) % heads_here
+    for i in range(block // lane):
+        rep = jnp.dot(
+            normed[:, i * lane:(i + 1) * lane], spread, preferred_element_type=jnp.float32
+        )
+        for g in range(heads_here):
+            xexp[g * all_rows:(g + 1) * all_rows, i * wide:(i + 1) * wide] = jnp.where(
+                which == g, rep, 0.0
+            ).astype(jnp.bfloat16)
+
+    flat_w = wbuf.reshape(qper + 2, depth, head)
+    span = min(depth, 2048)
+    stage1 = []
+    stage2 = []
+
+    def project(ch):
+        for j in (2 * ch, 2 * ch + 1):
+            weight_copies[j].wait()
+
+        def body(k, total):
+            cut = pl.ds(pl.multiple_of(k * span, span), span)
+            rhs = jnp.concatenate([flat_w[2 * ch, cut, :], flat_w[2 * ch + 1, cut, :]], axis=1)
+            return total + jnp.dot(xexp[:, cut], rhs, preferred_element_type=jnp.float32)
+
+        result = lax.fori_loop(
+            0, depth // span, body,
+            jnp.zeros((heads_here * all_rows, 2 * head), jnp.float32),
+        )
+        for g in range(heads_here):
+            for hh in range(hidden):
+                first = g * all_rows + hh * rows
+                part[ch, hh % 2, hh // 2, g] = result[first:first + rows, :]
+        copy = remote(
+            part.at[ch, 1 - c], recv1.at[ch], s1_send.at[ch], s1_sem.at[ch], z * 2 + 1 - c, m
+        )
+        copy.start()
+        stage1.append(copy)
+
+    def pass_on(ch):
+        stage1[ch].wait_recv()
+        part[ch, c] = part[ch, c] + recv1[ch]
+        for dz in range(1, zs):
+            zz = (z + dz) % zs
+            copy = remote(
+                part.at[ch, c, zz], recv2.at[ch, dz - 1],
+                s2_send.at[ch, dz - 1], s2_sem.at[ch, dz - 1], zz * 2 + c, m,
+            )
+            copy.start()
+            stage2.append(copy)
+
+    for ch in range(chunks):
+        project(ch)
+        if ch:
+            pass_on(ch - 1)
+    pass_on(chunks - 1)
+
+    cosine = trig[0]
+    sine = trig[1]
+
+    def rotated(values):
+        return values * cosine + pltpu.roll(values, head // 2, 1) * sine
+
+    for copy in stage2:
+        copy.wait_recv()
+
+    def summed(ch, g):
+        total = part[ch, c, z, g]
+        for dz in range(1, zs):
+            total = total + recv2[ch, dz - 1, g]
+        return total
+
+    seqs = kcache.shape[0]
+    steps = rows // seqs
+    many = qper * rows
+    row_id = lax.broadcasted_iota(jnp.int32, (many, 1), 0) % rows
+    row_seq = row_id // steps
+    row_step = row_id % steps
+    limit = jnp.concatenate([lens[...]] * qper, axis=0)[:, :1]
+    slot_ok = lax.broadcasted_iota(jnp.int32, (many, slots), 1) < limit
+    extra = lax.broadcasted_iota(jnp.int32, (many, head), 1)
+    fresh_ok = (extra // steps == row_seq) & (extra % steps <= row_step)
+    factor = head ** (-0.5)
+    rest = jnp.zeros((head - rows, head), jnp.float32)
+    nt = (((1,), (1,)), ((), ()))
+    head_sends = []
+    forwards = []
+
+    def attention(g):
+        kv = summed(0, g)
+        new_key = jnp.concatenate([rotated(kv[:, :head]), rest], axis=0).astype(jnp.bfloat16)
+        new_val = jnp.concatenate([kv[:, head:], rest], axis=0).astype(jnp.bfloat16)
+        queries = []
+        for ch in range(1, chunks):
+            both = summed(ch, g)
+            queries.append(rotated(both[:, :head]))
+            queries.append(rotated(both[:, head:]))
+        query = jnp.concatenate(queries, axis=0).astype(jnp.bfloat16)
+        for copy in cache_copies[g]:
+            copy.wait()
+        scores = None
+        for s in range(seqs):
+            one = lax.dot_general(query, kbuf[s, g], nt, preferred_element_type=jnp.float32)
+            scores = one if s == 0 else jnp.where(row_seq == s, one, scores)
+        scores = jnp.where(slot_ok, scores * factor, -jnp.inf)
+        fresh = lax.dot_general(query, new_key, nt, preferred_element_type=jnp.float32)
+        fresh = jnp.where(fresh_ok, fresh * factor, -jnp.inf)
+        top = jnp.maximum(
+            jnp.max(scores, axis=-1, keepdims=True), jnp.max(fresh, axis=-1, keepdims=True)
+        )
+        p = jnp.exp(scores - top)
+        p_fresh = jnp.exp(fresh - top)
+        total = jnp.sum(p, axis=-1, keepdims=True) + jnp.sum(p_fresh, axis=-1, keepdims=True)
+        weights = p.astype(jnp.bfloat16)
+        value = None
+        for s in range(seqs):
+            one = jnp.dot(weights, vbuf[s, g], preferred_element_type=jnp.float32)
+            value = one if s == 0 else jnp.where(row_seq == s, one, value)
+        value = value + jnp.dot(
+            p_fresh.astype(jnp.bfloat16), new_val, preferred_element_type=jnp.float32
+        )
+        value = value / total
+        line = jnp.concatenate([value[j * rows:(j + 1) * rows] for j in range(qper)], axis=1)
+        hbuf[g, c, z] = line.astype(jnp.bfloat16)
+        sends = []
+        for dz in range(1, zs):
+            zz = (z + dz) % zs
+            copy = remote(
+                hbuf.at[g, c, z], hbuf.at[g, c, z],
+                h_send.at[g, dz - 1], h_sem.at[g, z], zz * 2 + c, m,
+            )
+            copy.start()
+            sends.append(copy)
+        head_sends.append(sends)
+
+    def forward(g):
+        for dz in range(1, zs):
+            zz = (z + dz) % zs
+            arrived(hbuf.at[g, c, zz], h_sem.at[g, zz])
+        copy = remote(
+            hbuf.at[g, c], hbuf.at[g, c], f_send.at[g], f_sem.at[g], z * 2 + 1 - c, m
+        )
+        copy.start()
+        forwards.append(copy)
+
+    def multiply(g, cut):
+        lhs = hbuf[g].reshape(all_rows, qper * head)
+        return jnp.dot(lhs, obuf_w[g, :, cut], preferred_element_type=jnp.float32)
+
+    def gathered(g):
+        arrived(hbuf.at[g, 1 - c], f_sem.at[g])
+        out_copies[g].wait()
+
+    for g in range(heads_here):
+        attention(g)
+        if g:
+            forward(g - 1)
+    forward(heads_here - 1)
+
+    last = heads_here - 1
+    pieces = osend.shape[0]
+    narrow = width // pieces
+    for g in range(last):
+        gathered(g)
+        for n in range(pieces):
+            cut = slice(n * narrow, (n + 1) * narrow)
+            if g == 0:
+                acc[:, cut] = multiply(g, cut)
+            else:
+                acc[:, cut] += multiply(g, cut)
+    gathered(last)
+    zhalf = zs // mp
+    out_sends = []
+    for n in range(pieces):
+        cut = slice(n * narrow, (n + 1) * narrow)
+        block_sum = acc[:, cut] + multiply(last, cut)
+        for cc in range(2):
+            for zz in range(zs):
+                first = (cc * zs + zz) * rows
+                osend[n, zz // zhalf, zz % zhalf, cc] = block_sum[first:first + rows]
+        copy = remote(
+            osend.at[n, (m + 1) % mp], orecv.at[n], o_send.at[n], o_sem.at[n], h, (m + 1) % mp
+        )
+        copy.start()
+        out_sends.append(copy)
+    for n in range(pieces):
+        cut = slice(n * narrow, (n + 1) * narrow)
+        out_sends[n].wait_recv()
+        out[:, :, :, cut] = (osend[n, m] + orecv[n]).astype(out.dtype)
+
+    for copy, mine in row_sends:
+        if mine is None:
+            copy.wait_send()
+        else:
+
+            @pl.when(jnp.logical_not(mine))
+            def _(copy=copy):
+                copy.wait_send()
+
+    for copy in ss_sends + stage1 + stage2 + forwards + out_sends:
+        copy.wait_send()
+    for sends in head_sends:
+        for copy in sends:
+            copy.wait_send()
+
+
+def fused(
+    stream_rows, norm_gain, query_weight, keyval_weight, output_weight, key_cache, value_cache, lengths
+):
+    hidden = lax.axis_size("hidden")
+    mp = lax.axis_size("mp")
+    seqs, steps, narrow = stream_rows.shape
+    rows = seqs * steps
+    block, heads_here, q_width = query_weight.shape
+    head = key_cache.shape[3]
+    slots = key_cache.shape[2]
+    width = output_weight.shape[2]
+    nb = narrow // block
+    qper = q_width // head
+    chunks = (qper + 2) // 2
+    zs = hidden // 2
+    all_rows = hidden * rows
+    xb = jnp.transpose(stream_rows.reshape(rows, nb, block), (1, 0, 2))
+    gain = norm_gain.astype(jnp.float32).reshape(nb, 1, block)
+    half = head // 2
+    freq = jnp.exp(jnp.arange(half, dtype=jnp.float32) * (-2.0 * math.log(rope_base) / head))
+    pos = (lengths[:, None] + jnp.arange(steps, dtype=jnp.int32)[None, :]).astype(jnp.float32)
+    angle = pos.reshape(rows, 1) * freq
+    cosine = jnp.cos(angle)
+    sine = jnp.sin(angle)
+    trig = jnp.stack(
+        [jnp.concatenate([cosine, cosine], axis=1), jnp.concatenate([-sine, sine], axis=1)]
+    )
+    lens = jnp.broadcast_to(lengths[:, None, None], (seqs, steps, 128)).reshape(rows, 128)
+    f32, bf16, dma = jnp.float32, jnp.bfloat16, pltpu.SemaphoreType.DMA
+    pieces = 4
+    vmem = pl.BlockSpec(memory_space=pltpu.VMEM)
+    hbm = pl.BlockSpec(memory_space=pl.ANY)
+    out = pl.pallas_call(
+        functools.partial(fused_kernel, hidden=hidden, mp=mp, width=width),
+        out_shape=jax.ShapeDtypeStruct((zs // mp, 2, rows, width), bf16),
+        in_specs=[vmem] * 4 + [hbm] * 5,
+        out_specs=vmem,
+        scratch_shapes=[
+            pltpu.VMEM((hidden, rows, block), bf16),
+            pltpu.VMEM((rows, 128), f32),
+            pltpu.VMEM((mp, hidden, rows, 128), f32),
+            pltpu.VMEM((1, block), f32),
+            pltpu.VMEM((heads_here * all_rows, block * heads_here), bf16),
+            pltpu.VMEM((qper + 2, block, heads_here, head), bf16),
+            pltpu.VMEM((seqs, heads_here, slots, head), bf16),
+            pltpu.VMEM((seqs, heads_here, slots, head), bf16),
+            pltpu.VMEM((heads_here, q_width, width), bf16),
+            pltpu.VMEM((chunks, 2, zs, heads_here, rows, 2 * head), f32),
+            pltpu.VMEM((chunks, zs, heads_here, rows, 2 * head), f32),
+            pltpu.VMEM((chunks, zs - 1, heads_here, rows, 2 * head), f32),
+            pltpu.VMEM((heads_here, 2, zs, rows, q_width), bf16),
+            pltpu.VMEM((all_rows, width), f32),
+            pltpu.VMEM((pieces, mp, zs // mp, 2, rows, width // pieces), f32),
+            pltpu.VMEM((pieces, zs // mp, 2, rows, width // pieces), f32),
+            dma((nb * mp,)),
+            dma((hidden,)),
+            dma((hidden * mp,)),
+            dma((mp, hidden)),
+            dma((3,)),
+            dma((qper + 2,)),
+            dma((2, heads_here)),
+            dma((heads_here,)),
+            dma((chunks,)),
+            dma((chunks,)),
+            dma((chunks, zs - 1)),
+            dma((chunks, zs - 1)),
+            dma((heads_here, zs - 1)),
+            dma((heads_here, zs)),
+            dma((heads_here,)),
+            dma((heads_here,)),
+            dma((pieces,)),
+            dma((pieces,)),
+        ],
+        compiler_params=pltpu.CompilerParams(
+            collective_id=0, has_side_effects=True, vmem_limit_bytes=60 * 2**20
+        ),
+        name="fused_decode",
+    )(xb, gain, trig, lens, query_weight, keyval_weight, output_weight, key_cache, value_cache)
+    return out.reshape(zs // mp * 2 * seqs, steps, width)
+
+
 def solution(mesh):
     in_specs = (
         P(("groups", "hidden"), None, "mp"),
@@ -164,4 +599,6 @@
         P(("groups", "hidden")),
     )
     out_specs = P(("groups", "mp"), None, "hidden")
-    return jax.shard_map(local, mesh=mesh, in_specs=in_specs, out_specs=out_specs, check_vma=False)
+    fits = mesh.shape["hidden"] == 8 and mesh.shape["mp"] == 2
+    body = fused if fits else local
+    return jax.shard_map(body, mesh=mesh, in_specs=in_specs, out_specs=out_specs, check_vma=False)

time: 178 us -> 70.6 us (0.40)
  waiting for transfers between devices: 73.7 us -> 0 us
  Pallas kernels: 0 us -> 63.3 us
  matrix products: 27 us -> 0 us
  blocking collectives: 26.8 us -> 0 us
  local copies, waits for them, and re-layouts: 26.7 us -> 4.94 us
  between operations: 14.4 us -> 0.02 us
  starting transfers between devices: 5.35 us -> 0 us
    pallas_call x0 -> x1, Pallas kernels: none -> 63.3 us  [fused(): pl.pallas_call(functools.partial(fused_kernel, hidden=hidden, mp=mp, widt...]
    unnamed x3 -> x0, waiting for transfers between devices: 60 us -> none
    dot_general x11 -> x0, matrix products: 27 us -> none  [the longest x1 9.73 us: local(): product = jnp.dot(flat, wo_flat, preferred_element_type=jnp.float32)]
    all_gather x3 -> x0, blocking collectives: 26.8 us -> none  [the longest x1 14.8 us: local(): piece = lax.all_gather(heads_all, 'hidden', axis=0, tiled=True)]
    unnamed x16 -> x0, local copies, waits for them, and re-layouts: 20.8 us -> none
    reduce_scatter x1 -> x0, waiting for transfers between devices: 13.7 us -> none  [local(): lax.psum_scatter(partial_value, 'mp', scatter_dimension=0, tiled=True)]
    all_to_all x1 -> x0, starting transfers between devices: 5.09 us -> none  [local(): lax.all_to_all(normed, 'hidden', split_axis=0, concat_axis=0, tiled=True)]
    slice x5 -> x0, local copies, waits for them, and re-layouts: 1.89 us -> none  [the longest x1 0.92 us: local(): sums[..., :q_cols].reshape(seqs, steps_all, groups_here, per_group, head)]
  transfers between devices with their start and end apart: 3 -> 0, of which waited for: 2 -> 0; matrix products, arithmetic and copies ran while one was open for 12% -> 0% of each run, Pallas kernels for 0% -> 0%
where the time goes in v1:
time: 70.6 us; the launch traced here: 70.4 us
  Pallas kernels  63.3 us (90%)
  local copies, waits for them, and re-layouts  4.94 us (7%)
  other arithmetic  2.13 us (3%)
    pallas_call x1, Pallas kernels, fused(): pl.pallas_call(functools.partial(fused_kernel, hidden=hidden, mp=mp, widt...  63.3 us
    reshape x2, local copies, waits for them, and re-layouts, fused(): xb = jnp.transpose(stream_rows.reshape(rows, nb, block), (1, 0, 2))  1.72 us
    reshape x1, local copies, waits for them, and re-layouts, fused(): return out.reshape(zs // mp * 2 * seqs, steps, width)  1.66 us

profile of v1, /device:TPU:0, one launch (start us, length us, event | category | flops | bytes accessed | tf_op | source)
XLA Modules:
  0.0 70.4 jit_solution(8638885463633010710)
XLA Ops:
  0.0 0.7 %add.21 = s32[4,2]{1,0:T(4,128)S(1)} broadcast(s32[4]{0:T(128)} %param.15), dimensions={0} | broadcast | bytes 48 | tf_op jit(solution)/shard_map/add | solution.py:529
  0.7 0.1 add.22
  0.8 0.1 add.24
  0.9 0.7 broadcast_in_dim.2.lens
  1.6 0.1 multiply_cosine_fusion
  1.7 0.1 maximum_bitcast_fusion
  1.8 0.6 pad_maximum_fusion.trig
  2.4 1.3 %reshape.39 = f32[8192]{0:T(1024)} convert(bf16[8192]{0:T(1024)(128)(2,1)} %param.9) | non-fusion elementwise | flops 8192 | bytes 49152 | tf_op jit(solution)/shard_map/reshape | solution.py:526
  3.7 1.0 %reshape.35 = bf16[8,4,2048]{2,1,0:T(4,128)(2,1)S(1)} reshape(bf16[4,2,8192]{2,1,0:T(2,128)(2,1)} %param.8) | data formatting | bytes 262144 | tf_op jit(solution)/shard_map/reshape | solution.py:525
  4.7 0.7 %copy.11 = bf16[8,4,2048]{2,0,1:T(8,128)(2,1)} copy(bf16[8,4,2048]{2,1,0:T(4,128)(2,1)S(1)} %reshape.35) | data formatting | bytes 262144 | tf_op jit(solution)/shard_map/reshape | solution.py:525
  5.4 63.3 %fused_decode.1 = bf16[2,2,8,2048]{3,2,1,0:T(8,128)(2,1)} custom-call(bf16[4,8,2048]{2,1,0:T(8,128)(2,1)} %bitcast.10, f32[4,1,2048]{2,1,0:T(1,128)} %bitcast.11, f32[2,8,128]{2,1,0:T(8,128)} %pad_maximum_fusion.trig, s32[8,128]{1,0:T(8,128)} %broadcast_in_dim.2.lens, bf16[2048,4,1024]{2,1,0:T(4,128)(2,1)} %wq.1, bf16[2048,4,256]{2,1,0:T(4,128)(2,1)} %wkv.1, ...), custom_call_target="tpu_custom_call" | custom-call | tf_op jit(solution)/shard_map/fused_decode/pallas_call | solution.py:541
  68.7 1.7 %reshape.38 = bf16[16,2,2048]{2,1,0:T(2,128)(2,1)} reshape(bf16[2,2,8,2048]{3,2,1,0:T(8,128)(2,1)} %fused_decode.1) | data formatting | bytes 262144 | tf_op jit(solution)/shard_map/reshape | solution.py:587
  (3 shorter events, 0.0 us)

commit v2 on v1

--- a/solution.py
+++ b/solution.py
@@ -156,9 +156,9 @@
 
 
 def fused_kernel(
-    xb, gain, trig, lens, wq, wkv, wo, kcache, vcache, out,
-    xr, ssl, ssr, gbuf, xexp, wbuf, kbuf, vbuf, obuf_w, part, recv1, recv2, hbuf, acc, osend, orecv,
-    xsend_sem, xsem, ss_send, ss_sem, gsem, wsem, csem, wosem,
+    stream, gain, trig, wq, wkv, wo, kcache, vcache, out,
+    xr, ssl, ssr, xb, xexp, wbuf, kbuf, vbuf, obuf_w, part, recv1, recv2, hbuf, acc, osend, orecv,
+    xsend_sem, xsem, ss_sem, wsem, csem, wosem,
     s1_send, s1_sem, s2_send, s2_sem, h_send, h_sem, f_send, f_sem, o_send, o_sem,
     *, hidden, mp, width,
 ):
@@ -209,6 +209,19 @@
                 )
     pl.semaphore_wait(barrier, hidden * mp - 1)
 
+    stream_f = stream[...].astype(jnp.float32)
+    values = jnp.concatenate([stream_f[s] for s in range(stream.shape[0])], axis=0)
+    squares = jnp.sum(values * values, axis=-1, keepdims=True)
+    ssl[...] = jnp.broadcast_to(squares, ssl.shape)
+    ss_copy = remote(ssl, ssr, ss_sem.at[0], ss_sem.at[1], h, (m + 1) % mp)
+    ss_copy.start()
+    ss_copy.wait_recv()
+    total_sq = ssl[...] + ssr[...]
+    scale = lax.rsqrt(total_sq / (nb * mp * block) + 1e-05)[:, :1]
+    normed_here = values * scale * gain[...].astype(jnp.float32)
+    for b in range(nb):
+        xb[b] = normed_here[:, b * block:(b + 1) * block].astype(jnp.bfloat16)
+
     row_sends = []
     for b in range(nb):
         for dm in range(mp):
@@ -234,30 +247,6 @@
                 copy.start()
                 row_sends.append((copy, None))
 
-    holder = h // nb == m
-    gain_copy = remote(gain.at[h % nb], gbuf, gsem.at[0], gsem.at[1], h, (m + 1) % mp)
-    gain_local = pltpu.make_async_copy(gain.at[h % nb], gbuf, gsem.at[2])
-
-    @pl.when(holder)
-    def _():
-        gain_copy.start()
-        gain_local.start()
-
-    values = xb[...].astype(jnp.float32)
-    squares = jnp.sum(jnp.sum(values * values, axis=0), axis=-1, keepdims=True)
-    ssl[...] = jnp.broadcast_to(squares, ssl.shape)
-    ssr[m, h] = ssl[...]
-    ss_sends = []
-    for dh in range(hidden):
-        for dm in range(mp):
-            if dh or dm:
-                copy = remote(
-                    ssl, ssr.at[m, h], ss_send.at[dh * mp + dm], ss_sem.at[m, h],
-                    (h + dh) % hidden, (m + dm) % mp,
-                )
-                copy.start()
-                ss_sends.append(copy)
-
     cache_copies = []
     for g in range(heads_here):
         pair = (
@@ -273,28 +262,9 @@
         copy.start()
         out_copies.append(copy)
 
-    for dh in range(hidden):
-        for dm in range(mp):
-            if dh or dm:
-                hh = (h + dh) % hidden
-                mm = (m + dm) % mp
-                arrived(ssr.at[mm, hh], ss_sem.at[mm, hh])
-
-    @pl.when(holder)
-    def _():
-        gain_local.wait()
-        gain_copy.wait_send()
-
-    @pl.when(jnp.logical_not(holder))
-    def _():
-        gain_copy.wait_recv()
-
     for src in range(hidden):
         arrived(xr.at[src], xsem.at[src])
-    total_sq = jnp.sum(ssr[...], axis=0).reshape(all_rows, ssl.shape[1])
-    scale = lax.rsqrt(total_sq / (nb * mp * block) + 1e-05)[:, :1]
-    rows_f = xr[...].astype(jnp.float32).reshape(all_rows, block)
-    normed = (rows_f * scale * gbuf[...]).astype(jnp.bfloat16)
+    normed = xr[...].astype(jnp.float32).reshape(all_rows, block).astype(jnp.bfloat16)
 
     lane = 128
     wide = lane * heads_here
@@ -378,8 +348,8 @@
     row_id = lax.broadcasted_iota(jnp.int32, (many, 1), 0) % rows
     row_seq = row_id // steps
     row_step = row_id % steps
-    limit = jnp.concatenate([lens[...]] * qper, axis=0)[:, :1]
-    slot_ok = lax.broadcasted_iota(jnp.int32, (many, slots), 1) < limit
+    limit = jnp.concatenate([trig[2]] * qper, axis=0)[:, :1]
+    slot_ok = lax.broadcasted_iota(jnp.int32, (many, slots), 1).astype(jnp.float32) < limit
     extra = lax.broadcasted_iota(jnp.int32, (many, head), 1)
     fresh_ok = (extra // steps == row_seq) & (extra % steps <= row_step)
     factor = head ** (-0.5)
@@ -499,7 +469,7 @@
             def _(copy=copy):
                 copy.wait_send()
 
-    for copy in ss_sends + stage1 + stage2 + forwards + out_sends:
+    for copy in [ss_copy] + stage1 + stage2 + forwards + out_sends:
         copy.wait_send()
     for sends in head_sends:
         for copy in sends:
@@ -522,18 +492,18 @@
     chunks = (qper + 2) // 2
     zs = hidden // 2
     all_rows = hidden * rows
-    xb = jnp.transpose(stream_rows.reshape(rows, nb, block), (1, 0, 2))
-    gain = norm_gain.astype(jnp.float32).reshape(nb, 1, block)
+    gain = norm_gain.reshape(1, narrow)
     half = head // 2
     freq = jnp.exp(jnp.arange(half, dtype=jnp.float32) * (-2.0 * math.log(rope_base) / head))
-    pos = (lengths[:, None] + jnp.arange(steps, dtype=jnp.int32)[None, :]).astype(jnp.float32)
-    angle = pos.reshape(rows, 1) * freq
-    cosine = jnp.cos(angle)
-    sine = jnp.sin(angle)
-    trig = jnp.stack(
-        [jnp.concatenate([cosine, cosine], axis=1), jnp.concatenate([-sine, sine], axis=1)]
-    )
-    lens = jnp.broadcast_to(lengths[:, None, None], (seqs, steps, 128)).reshape(rows, 128)
+    filled = jnp.broadcast_to(lengths[:, None], (seqs, steps)).reshape(rows, 1)
+    step_of = jnp.arange(rows, dtype=jnp.int32)[:, None] % steps
+    angle = (filled + step_of).astype(jnp.float32) * jnp.concatenate([freq, freq])
+    sign = jnp.where(jnp.arange(head) < half, -1.0, 1.0)
+    kind = jnp.arange(3)[:, None, None]
+    trig = jnp.where(
+        kind == 0, jnp.cos(angle),
+        jnp.where(kind == 1, sign * jnp.sin(angle), filled.astype(jnp.float32)),
+    )
     f32, bf16, dma = jnp.float32, jnp.bfloat16, pltpu.SemaphoreType.DMA
     pieces = 4
     vmem = pl.BlockSpec(memory_space=pltpu.VMEM)
@@ -541,13 +511,13 @@
     out = pl.pallas_call(
         functools.partial(fused_kernel, hidden=hidden, mp=mp, width=width),
         out_shape=jax.ShapeDtypeStruct((zs // mp, 2, rows, width), bf16),
-        in_specs=[vmem] * 4 + [hbm] * 5,
+        in_specs=[vmem] * 3 + [hbm] * 5,
         out_specs=vmem,
         scratch_shapes=[
             pltpu.VMEM((hidden, rows, block), bf16),
             pltpu.VMEM((rows, 128), f32),
-            pltpu.VMEM((mp, hidden, rows, 128), f32),
-            pltpu.VMEM((1, block), f32),
+            pltpu.VMEM((rows, 128), f32),
+            pltpu.VMEM((nb, rows, block), bf16),
             pltpu.VMEM((heads_here * all_rows, block * heads_here), bf16),
             pltpu.VMEM((qper + 2, block, heads_here, head), bf16),
             pltpu.VMEM((seqs, heads_here, slots, head), bf16),
@@ -562,9 +532,7 @@
             pltpu.VMEM((pieces, zs // mp, 2, rows, width // pieces), f32),
             dma((nb * mp,)),
             dma((hidden,)),
-            dma((hidden * mp,)),
-            dma((mp, hidden)),
-            dma((3,)),
+            dma((2,)),
             dma((qper + 2,)),
             dma((2, heads_here)),
             dma((heads_here,)),
@@ -583,7 +551,7 @@
             collective_id=0, has_side_effects=True, vmem_limit_bytes=60 * 2**20
         ),
         name="fused_decode",
-    )(xb, gain, trig, lens, query_weight, keyval_weight, output_weight, key_cache, value_cache)
+    )(stream_rows, gain, trig, query_weight, keyval_weight, output_weight, key_cache, value_cache)
     return out.reshape(zs // mp * 2 * seqs, steps, width)
 
 

time: 70.6 us -> 66.9 us (0.948)
  Pallas kernels: 63.3 us -> 61.9 us
  other arithmetic: 2.13 us -> 0.89 us
  local copies, waits for them, and re-layouts: 4.94 us -> 3.83 us
    pallas_call x1, Pallas kernels: 63.3 us -> 61.9 us  [fused(): pl.pallas_call(functools.partial(fused_kernel, hidden=hidden, mp=mp, widt...]
    reshape x1 -> x0, other arithmetic: 1.33 us -> none  [fused(): gain = norm_gain.astype(jnp.float32).reshape(nb, 1, block)]
    add x4 -> x0, local copies, waits for them, and re-layouts: 0.9 us -> none  [fused(): lengths[:, None] + jnp.arange(steps, dtype=jnp.int32)[None, :]]
    select_n x0 -> x2, other arithmetic: none -> 0.76 us  [the longest x1 0.68 us: fused(): jnp.where(kind == 0, jnp.cos(angle), jnp.where(kind == 1, sign * jnp.sin(...]
where the time goes in v2:
time: 66.9 us; the launch traced here: 66.6 us
  Pallas kernels  61.9 us (93%)
  local copies, waits for them, and re-layouts  3.83 us (6%)
  other arithmetic  0.89 us (1%)
    pallas_call x1, Pallas kernels, fused(): pl.pallas_call(functools.partial(fused_kernel, hidden=hidden, mp=mp, widt...  61.9 us
    reshape x1, local copies, waits for them, and re-layouts, fused(): return out.reshape(zs // mp * 2 * seqs, steps, width)  1.66 us
    reshape x1, local copies, waits for them, and re-layouts, fused(): gain = norm_gain.reshape(1, narrow)  1.35 us

profile of v2, /device:TPU:0, one launch (start us, length us, event | category | flops | bytes accessed | tf_op | source)
XLA Modules:
  0.0 66.6 jit_solution(277187579532296426)
XLA Ops:
  0.0 0.1 compare_select_fusion
  0.1 0.7 %broadcast_in_dim.51 = s32[4,2]{1,0:T(4,128)S(1)} broadcast(s32[4]{0:T(128)} %param.15), dimensions={0} | broadcast | bytes 48 | tf_op jit(solution)/shard_map/broadcast_in_dim | solution.py:498
  0.8 0.1 reshape.56
  0.9 0.1 multiply_cosine_fusion
  1.0 0.7 %select_select_fusion.trig = f32[3,8,128]{2,1,0:T(8,128)} fusion(f32[8]{0:T(128)S(1)} %get-tuple-element.8, f32[8,128]{1,0:T(8,128)S(1)} %get-tuple-element.6, f32[8,128]{1,0:T(8,128)S(1)} %get-tuple-element.5, pred[3]{0:T(512)(128)(4,1)S(1)} %get-tuple-element.11, pred[3]{0:T(512)(128)(4,1)S(1)} %get-tuple-element.12), kind=kLoop, calls=%fused_computation | loop fusion | flops 6144 | bytes 20518 | tf_op jit(solution)/shard_map/jit(_where)/select_n | solution.py:503
  1.7 1.3 %reshape.55.gain = bf16[1,8192]{1,0:T(2,128)(2,1)} reshape(bf16[8192]{0:T(1024)(128)(2,1)} %param.9) | data formatting | bytes 32768 | tf_op jit(solution)/shard_map/reshape | solution.py:495
  3.1 61.9 %fused_decode.1 = bf16[2,2,8,2048]{3,2,1,0:T(8,128)(2,1)} custom-call(bf16[4,2,8192]{2,1,0:T(2,128)(2,1)} %stream.1, bf16[1,8192]{1,0:T(2,128)(2,1)} %reshape.55.gain, f32[3,8,128]{2,1,0:T(8,128)} %select_select_fusion.trig, bf16[2048,4,1024]{2,1,0:T(4,128)(2,1)} %wq.1, bf16[2048,4,256]{2,1,0:T(4,128)(2,1)} %wkv.1, bf16[4,1024,2048]{2,1,0:T(8,128)(2,1)} %wo.1, ...), custom_call_target="tpu_custom_call" | custom-call | tf_op jit(solution)/shard_map/fused_decode/pallas_call | solution.py:511
  65.0 1.7 %reshape.57 = bf16[16,2,2048]{2,1,0:T(2,128)(2,1)} reshape(bf16[2,2,8,2048]{3,2,1,0:T(8,128)(2,1)} %fused_decode.1) | data formatting | bytes 262144 | tf_op jit(solution)/shard_map/reshape | solution.py:555
  (3 shorter events, 0.0 us)

commit v3 on v2

--- a/solution.py
+++ b/solution.py
@@ -157,7 +157,7 @@
 
 def fused_kernel(
     stream, gain, trig, wq, wkv, wo, kcache, vcache, out,
-    xr, ssl, ssr, xb, xexp, wbuf, kbuf, vbuf, obuf_w, part, recv1, recv2, hbuf, acc, osend, orecv,
+    xr, ssl, ssr, xb, xexp, wbuf, kbuf, vbuf, obuf_w, part, recv1, recv2, hbuf, acc, osend, olink, orecv,
     xsend_sem, xsem, ss_sem, wsem, csem, wosem,
     s1_send, s1_sem, s2_send, s2_sem, h_send, h_sem, f_send, f_sem, o_send, o_sem,
     *, hidden, mp, width,
@@ -450,15 +450,16 @@
             for zz in range(zs):
                 first = (cc * zs + zz) * rows
                 osend[n, zz // zhalf, zz % zhalf, cc] = block_sum[first:first + rows]
+                olink[n, zz // zhalf, zz % zhalf, cc] = block_sum[first:first + rows].astype(olink.dtype)
         copy = remote(
-            osend.at[n, (m + 1) % mp], orecv.at[n], o_send.at[n], o_sem.at[n], h, (m + 1) % mp
+            olink.at[n, (m + 1) % mp], orecv.at[n], o_send.at[n], o_sem.at[n], h, (m + 1) % mp
         )
         copy.start()
         out_sends.append(copy)
     for n in range(pieces):
         cut = slice(n * narrow, (n + 1) * narrow)
         out_sends[n].wait_recv()
-        out[:, :, :, cut] = (osend[n, m] + orecv[n]).astype(out.dtype)
+        out[:, :, :, cut] = (osend[n, m] + orecv[n].astype(jnp.float32)).astype(out.dtype)
 
     for copy, mine in row_sends:
         if mine is None:
@@ -529,7 +530,8 @@
             pltpu.VMEM((heads_here, 2, zs, rows, q_width), bf16),
             pltpu.VMEM((all_rows, width), f32),
             pltpu.VMEM((pieces, mp, zs // mp, 2, rows, width // pieces), f32),
-            pltpu.VMEM((pieces, zs // mp, 2, rows, width // pieces), f32),
+            pltpu.VMEM((pieces, mp, zs // mp, 2, rows, width // pieces), bf16),
+            pltpu.VMEM((pieces, zs // mp, 2, rows, width // pieces), bf16),
             dma((nb * mp,)),
             dma((hidden,)),
             dma((2,)),

time: 66.9 us -> 64.2 us (0.960)
  Pallas kernels: 61.9 us -> 59.2 us
    pallas_call x1, Pallas kernels: 61.9 us -> 59.2 us  [fused(): pl.pallas_call(functools.partial(fused_kernel, hidden=hidden, mp=mp, widt...]
where the time goes in v3:
time: 64.2 us; the launch traced here: 63.9 us
  Pallas kernels  59.2 us (92%)
  local copies, waits for them, and re-layouts  3.83 us (6%)
  other arithmetic  0.89 us (1%)
    pallas_call x1, Pallas kernels, fused(): pl.pallas_call(functools.partial(fused_kernel, hidden=hidden, mp=mp, widt...  59.2 us
    reshape x1, local copies, waits for them, and re-layouts, fused(): return out.reshape(zs // mp * 2 * seqs, steps, width)  1.66 us
    reshape x1, local copies, waits for them, and re-layouts, fused(): gain = norm_gain.reshape(1, narrow)  1.35 us

profile of v3, /device:TPU:0, one launch (start us, length us, event | category | flops | bytes accessed | tf_op | source)
XLA Modules:
  0.0 63.9 jit_solution(7207174930177752352)
XLA Ops:
  0.0 0.1 compare_select_fusion
  0.1 0.7 %broadcast_in_dim.51 = s32[4,2]{1,0:T(4,128)S(1)} broadcast(s32[4]{0:T(128)} %param.15), dimensions={0} | broadcast | bytes 48 | tf_op jit(solution)/shard_map/broadcast_in_dim | solution.py:499
  0.8 0.1 reshape.56
  0.9 0.1 multiply_cosine_fusion
  1.0 0.7 %select_select_fusion.trig = f32[3,8,128]{2,1,0:T(8,128)} fusion(f32[8]{0:T(128)S(1)} %get-tuple-element.8, f32[8,128]{1,0:T(8,128)S(1)} %get-tuple-element.6, f32[8,128]{1,0:T(8,128)S(1)} %get-tuple-element.5, pred[3]{0:T(512)(128)(4,1)S(1)} %get-tuple-element.11, pred[3]{0:T(512)(128)(4,1)S(1)} %get-tuple-element.12), kind=kLoop, calls=%fused_computation | loop fusion | flops 6144 | bytes 20518 | tf_op jit(solution)/shard_map/jit(_where)/select_n | solution.py:504
  1.7 1.3 %reshape.55.gain = bf16[1,8192]{1,0:T(2,128)(2,1)} reshape(bf16[8192]{0:T(1024)(128)(2,1)} %param.9) | data formatting | bytes 32768 | tf_op jit(solution)/shard_map/reshape | solution.py:496
  3.1 59.2 %fused_decode.1 = bf16[2,2,8,2048]{3,2,1,0:T(8,128)(2,1)} custom-call(bf16[4,2,8192]{2,1,0:T(2,128)(2,1)} %stream.1, bf16[1,8192]{1,0:T(2,128)(2,1)} %reshape.55.gain, f32[3,8,128]{2,1,0:T(8,128)} %select_select_fusion.trig, bf16[2048,4,1024]{2,1,0:T(4,128)(2,1)} %wq.1, bf16[2048,4,256]{2,1,0:T(4,128)(2,1)} %wkv.1, bf16[4,1024,2048]{2,1,0:T(8,128)(2,1)} %wo.1, ...), custom_call_target="tpu_custom_call" | custom-call | tf_op jit(solution)/shard_map/fused_decode/pallas_call | solution.py:512
  62.3 1.7 %reshape.57 = bf16[16,2,2048]{2,1,0:T(2,128)(2,1)} reshape(bf16[2,2,8,2048]{3,2,1,0:T(8,128)(2,1)} %fused_decode.1) | data formatting | bytes 262144 | tf_op jit(solution)/shard_map/reshape | solution.py:557
  (3 shorter events, 0.0 us)
